TPU v7x, 32 devices: a whole 2x2x4 slice. The times are simulated.
32 devices in a mesh: ens: 2 (over x), tile: 16 (over z, y, core).
Axes of the slice: x: 2, y: 2, z: 4, core: 2. Of those that a mesh axis runs over, the one named last changes fastest.
Arguments:
- atmosphere: bfloat16 [256, 256, 128], P(('ens', 'tile')), parts along dimension 0, may hold values from -6 to 6
- ocean_state: bfloat16 [4096, 512], P(('ens', 'tile')), parts along dimension 0, may hold values from -6 to 6
- land_sea: int32 [2048], P('tile'), may hold values 0 or 1
- owners: int32 [2048, 1], P('tile'), may hold values from 0 to 15; in each aligned block of 128 rows (0 to 127, 128 to 255, ...) at most 16 rows name the same one
- rotations: int32 [16], replicated, may hold values from 0 to 255
- conv_weight: bfloat16 [3, 9, 128, 128], replicated, may hold values from -0.1875 to 0.1875
- conv_bias: bfloat16 [3, 128], replicated, may hold values from -3 to 3
- force_weight: bfloat16 [128, 32], replicated, may hold values from -0.5 to 0.5
- ocean_weight: bfloat16 [16, 9, 64, 32], P('tile'), may hold values from -0.25 to 0.25
Outputs:
- atmos_out: bfloat16 [256, 256, 128], P(('ens', 'tile')), parts along dimension 0
- sea_state: bfloat16 [4096, 512], P(('ens', 'tile')), parts along dimension 0
There are 2 independent parts, one for each index of `ens`. A program takes and returns all parts, laid end to end along the dimension named above; an argument that names none is the same for every part. Nothing has to cross between parts.
Inputs may be any that keep to these rules, and one draw needn't show every extreme that they name: `owners`: among the 128 blocks of one band no owner appears more than 16 times, and some owner appears exactly 16 times.
All inputs are finite; a program needn't handle non-finite values. No bound on the sum of `land_sea` on one device may be relied on, other than what follows from the above.
Results may differ from a plain program's by a relative error of at most 0.009.
Values may be sent and summed in bfloat16 or wider, within the bound.
A program may use at most 64 MiB of HBM per device.

v0:
```python
import functools
import jax
import jax.numpy as jnp
from jax import lax
from jax.experimental import pallas as pl
from jax.experimental.pallas import tpu as pltpu
from jax.sharding import PartitionSpec as P

LEADS = 2
LAYERS = 3
BH = 4
BW = 4
MARGIN = 2**LAYERS - 1
VMEM_LIMIT = 48 * 1024 * 1024


def one_hot(mask):
    return jnp.where(mask, 1.0, 0.0).astype(jnp.bfloat16)


def moved(matrix, values):
    return jnp.dot(matrix, values, preferred_element_type=jnp.float32).astype(jnp.bfloat16)


def atmosphere_kernel(
    tile_count, rot_ref, band_ref, w_ref, bias_ref, lead1_ref, lead2_ref,
    ext, mid1, mid2, taps, send_sem, recv_sem,
):
    me = lax.axis_index("tile")
    rows, columns, channels = band_ref.shape
    has_up = me > 0
    has_down = me < tile_count - 1
    barrier = pltpu.get_barrier_semaphore()

    @pl.when(has_up)
    def _():
        pl.semaphore_signal(barrier, inc=1, device_id={"tile": me - 1})

    @pl.when(has_down)
    def _():
        pl.semaphore_signal(barrier, inc=1, device_id={"tile": me + 1})

    shift = rot_ref[me]
    to = lax.broadcasted_iota(jnp.int32, (columns, columns), 0)
    source = lax.broadcasted_iota(jnp.int32, (columns, columns), 1)
    distance = source - to + shift
    turn = one_hot((distance == 0) | (distance == columns))
    for r in range(rows):
        ext[0, MARGIN + r] = moved(turn, band_ref[r])

    pl.semaphore_wait(barrier, jnp.minimum(me, 1) + jnp.minimum(tile_count - 1 - me, 1))

    def copies(lead):
        up = pltpu.make_async_remote_copy(
            src_ref=ext.at[lead, pl.ds(MARGIN, MARGIN)],
            dst_ref=ext.at[lead, pl.ds(MARGIN + rows, MARGIN)],
            send_sem=send_sem.at[lead, 0],
            recv_sem=recv_sem.at[lead, 0],
            device_id={"tile": me - 1},
        )
        down = pltpu.make_async_remote_copy(
            src_ref=ext.at[lead, pl.ds(rows, MARGIN)],
            dst_ref=ext.at[lead, pl.ds(0, MARGIN)],
            send_sem=send_sem.at[lead, 1],
            recv_sem=recv_sem.at[lead, 1],
            device_id={"tile": me + 1},
        )
        return up, down

    def start(lead):
        up, down = copies(lead)

        @pl.when(has_up)
        def _():
            up.start()

        @pl.when(has_down)
        def _():
            down.start()

    def finish(lead):
        up, down = copies(lead)

        @pl.when(has_up)
        def _():
            down.wait_recv()

        @pl.when(has_down)
        def _():
            up.wait_recv()

    def layer(index, source_of, store, out_rows, margin_left):
        dilation = 2**index
        bias = bias_ref[pl.ds(index, 1), :].astype(jnp.float32)

        def pair(g, carry):
            r = (g // dilation) * (2 * dilation) + g % dilation
            lhs = jnp.concatenate([source_of(r + k * dilation) for k in range(4)], axis=1)
            y = jnp.dot(lhs, taps[index], preferred_element_type=jnp.float32)
            for o in range(2):
                base = o * 3 * channels
                total = (
                    pltpu.roll(y[:, base : base + channels], dilation, 0)
                    + y[:, base + channels : base + 2 * channels]
                    + pltpu.roll(
                        y[:, base + 2 * channels : base + 3 * channels], columns - dilation, 0
                    )
                )
                row = r + o * dilation
                centre = lhs[:, (1 + o) * channels : (2 + o) * channels].astype(jnp.float32)
                value = centre + jax.nn.gelu(total + bias)
                if margin_left:
                    position = me * rows - margin_left + row
                    inside = (position >= 0) & (position < tile_count * rows)
                    value = jnp.where(inside, value, 0.0)
                store(row, value.astype(jnp.bfloat16))
            return carry

        lax.fori_loop(0, out_rows // 2, pair, 0, unroll=2)

    start(0)

    for index in range(LAYERS):
        for k in range(4):
            for o in range(2):
                for b in range(3):
                    a = k - o
                    where = (
                        index,
                        pl.ds(k * channels, channels),
                        pl.ds((o * 3 + b) * channels, channels),
                    )
                    if 0 <= a <= 2:
                        taps[where] = w_ref[index, a * 3 + b]
                    else:
                        taps[where] = jnp.zeros((channels, channels), jnp.bfloat16)

    @pl.when(jnp.logical_not(has_up))
    def _():
        for lead in range(LEADS):
            for r in range(MARGIN):
                ext[lead, r] = jnp.zeros((columns, channels), jnp.bfloat16)

    @pl.when(jnp.logical_not(has_down))
    def _():
        for lead in range(LEADS):
            for r in range(MARGIN):
                ext[lead, MARGIN + rows + r] = jnp.zeros((columns, channels), jnp.bfloat16)

    def set_mid1(row, value):
        mid1[row] = value

    def set_mid2(row, value):
        mid2[row] = value

    def set_lead1(row, value):
        lead1_ref[row] = value
        ext[1, MARGIN + row] = value

    def set_lead2(row, value):
        lead2_ref[row] = value

    for lead in range(LEADS):
        finish(lead)
        layer(0, lambda r, lead=lead: ext[lead, r], set_mid1, rows + 12, 6)
        layer(1, lambda r: mid1[r], set_mid2, rows + 8, 4)
        layer(2, lambda r: mid2[r], (set_lead1, set_lead2)[lead], rows, 0)
        if lead + 1 < LEADS:
            start(lead + 1)

    for lead in range(LEADS):
        up, down = copies(lead)

        @pl.when(has_up)
        def _():
            up.wait_send()

        @pl.when(has_down)
        def _():
            down.wait_send()


def atmosphere_leads(tile_count, rotations, band, conv_weight, conv_bias):
    rows, columns, channels = band.shape
    vmem = pl.BlockSpec(memory_space=pltpu.VMEM)
    extended = (rows + 2 * MARGIN, columns, channels)
    return pl.pallas_call(
        functools.partial(atmosphere_kernel, tile_count),
        out_shape=[jax.ShapeDtypeStruct(band.shape, jnp.bfloat16)] * 2,
        in_specs=[pl.BlockSpec(memory_space=pltpu.SMEM), vmem, vmem, vmem],
        out_specs=[vmem, vmem],
        scratch_shapes=[
            pltpu.VMEM((LEADS, *extended), jnp.bfloat16),
            pltpu.VMEM((rows + 12, columns, channels), jnp.bfloat16),
            pltpu.VMEM((rows + 8, columns, channels), jnp.bfloat16),
            pltpu.VMEM((LAYERS, 4 * channels, 6 * channels), jnp.bfloat16),
            pltpu.SemaphoreType.DMA((LEADS, 2)),
            pltpu.SemaphoreType.DMA((LEADS, 2)),
        ],
        compiler_params=pltpu.CompilerParams(
            collective_id=0, has_side_effects=True, vmem_limit_bytes=VMEM_LIMIT
        ),
        cost_estimate=pl.CostEstimate(
            flops=2 * 88 * columns * 9 * channels * channels,
            bytes_accessed=4 * rows * columns * channels * 2,
            transcendentals=88 * columns * channels,
        ),
        name="atmosphere",
    )(rotations, band, conv_weight, conv_bias)


def ocean_kernel(
    tile_count, rot_ref, lead1_ref, lead2_ref, state_ref, land_ref, owner_ref, fw_ref, v_ref,
    atmos_ref, sea_ref, lhs, rhs, total,
):
    me = lax.axis_index("tile")
    rows, columns, channels = lead1_ref.shape
    blocks, width = state_ref.shape
    ocean_ch = fw_ref.shape[1]
    cells = BH * BW
    group = BW * ocean_ch
    across = columns // BW
    shift = rot_ref[me]

    to = lax.broadcasted_iota(jnp.int32, (columns, columns), 0)
    source = lax.broadcasted_iota(jnp.int32, (columns, columns), 1)
    distance = to + shift - source
    back = one_hot((distance == 0) | (distance == columns))
    for r in range(rows):
        atmos_ref[r] = moved(back, lead2_ref[r])

    distance = (to % across) * BW + to // across + shift - source
    gather = one_hot((distance == 0) | (distance == columns))
    lane = lax.broadcasted_iota(jnp.int32, (ocean_ch, group), 1)
    spread = one_hot(lane % ocean_ch == lax.broadcasted_iota(jnp.int32, (ocean_ch, group), 0))
    fw4 = moved(fw_ref[...], spread)

    s = lax.broadcasted_iota(jnp.int32, (width, width), 0)
    t = lax.broadcasted_iota(jnp.int32, (width, width), 1)
    permute = one_hot((s // cells == t % ocean_ch) & (s % cells == t // ocean_ch))
    state = moved(state_ref[...], permute)

    piece_lane = lax.broadcasted_iota(jnp.int32, (across, group), 1) // ocean_ch
    lhs[...] = jnp.zeros_like(lhs)
    wide = 2 * group
    for r in range(rows):
        i, pr = r // BH, r % BH
        forcing = 0.5 * (
            jnp.dot(lead1_ref[r], fw4, preferred_element_type=jnp.float32)
            + jnp.dot(lead2_ref[r], fw4, preferred_element_type=jnp.float32)
        )
        y = jnp.dot(gather, forcing.astype(jnp.bfloat16), preferred_element_type=jnp.float32)
        piece = jnp.zeros((across, group), jnp.float32)
        for pc in range(BW):
            piece = jnp.where(piece_lane == pc, y[pc * across : (pc + 1) * across], piece)
        piece = piece.astype(jnp.bfloat16)
        for a in range(3):
            q = pr + 1 - a
            if 0 <= q < BH:
                lhs[pl.ds(q * blocks + i * across, across), pl.ds(a * wide, group)] = piece
    for pr in range(BH):
        for a in range(3):
            q = pr + 1 - a
            if 0 <= q < BH:
                lhs[pl.ds(q * blocks, blocks), pl.ds(a * wide + group, group)] = state[
                    :, pr * group : (pr + 1) * group
                ]

    owner = jnp.concatenate([jnp.broadcast_to(owner_ref[...], (blocks, group))] * BH, axis=0)
    total[...] = jnp.zeros_like(total)
    v_lane = lax.broadcasted_iota(jnp.int32, (v_ref.shape[1], group), 1) // ocean_ch

    def two_owners(k, carry):
        for half in range(2):
            v = v_ref[2 * k + half].astype(jnp.float32)
            for pc in range(BW):
                turned = v if pc == 1 else pltpu.roll(v, ((pc - 1) * ocean_ch) % group, 1)
                if pc == 0:
                    turned = jnp.where(v_lane == BW - 1, 0.0, turned)
                if pc > 2:
                    turned = jnp.where(v_lane < pc - 1, 0.0, turned)
                turned = turned.astype(jnp.bfloat16)
                for ah in range(6):
                    rhs[
                        pl.ds(ah * group + pc * ocean_ch, ocean_ch), pl.ds(half * group, group)
                    ] = turned[ah * ocean_ch : (ah + 1) * ocean_ch]
        y = jnp.dot(lhs[...], rhs[...], preferred_element_type=jnp.float32)
        kept = jnp.where(owner == 2 * k, y[:, :group], total[...])
        total[...] = jnp.where(owner == 2 * k + 1, y[:, group:], kept)
        return carry

    lax.fori_loop(0, tile_count // 2, two_owners, 0)

    sea = jnp.broadcast_to(land_ref[...], (blocks, group)) > 0
    out = jnp.zeros((blocks, width), jnp.float32)
    t = lax.broadcasted_iota(jnp.int32, (group, width), 0)
    s = lax.broadcasted_iota(jnp.int32, (group, width), 1)
    for q in range(BH):
        old = state[:, q * group : (q + 1) * group].astype(jnp.float32)
        new = old + jax.nn.gelu(total[pl.ds(q * blocks, blocks), :])
        new = jnp.where(sea, new, 0.0).astype(jnp.bfloat16)
        tq = t + q * group
        unpermute = one_hot((s // cells == tq % ocean_ch) & (s % cells == tq // ocean_ch))
        out = out + jnp.dot(new, unpermute, preferred_element_type=jnp.float32)
    sea_ref[...] = out.astype(jnp.bfloat16)


def ocean_step(tile_count, rotations, lead1, lead2, state, land, owners, force_weight, gathered):
    vmem = pl.BlockSpec(memory_space=pltpu.VMEM)
    blocks = state.shape[0]
    group = BW * force_weight.shape[1]
    return pl.pallas_call(
        functools.partial(ocean_kernel, tile_count),
        out_shape=[
            jax.ShapeDtypeStruct(lead1.shape, jnp.bfloat16),
            jax.ShapeDtypeStruct(state.shape, jnp.bfloat16),
        ],
        in_specs=[pl.BlockSpec(memory_space=pltpu.SMEM)] + [vmem] * 7,
        out_specs=[vmem, vmem],
        scratch_shapes=[
            pltpu.VMEM((BH * blocks, 6 * group), jnp.bfloat16),
            pltpu.VMEM((6 * group, 2 * group), jnp.bfloat16),
            pltpu.VMEM((BH * blocks, group), jnp.float32),
        ],
        compiler_params=pltpu.CompilerParams(vmem_limit_bytes=VMEM_LIMIT),
        name="ocean",
    )(rotations, lead1, lead2, state, land, owners, force_weight, gathered)


def local(
    tile_count, atmosphere, ocean_state, land_sea, owners, rotations, conv_weight, conv_bias,
    force_weight, ocean_weight,
):
    joined_ch, ocean_ch = ocean_weight.shape[2:]
    own = ocean_weight[0].reshape(3, 3, joined_ch, ocean_ch)[:, ::-1].transpose(0, 2, 1, 3)
    own = jnp.pad(own, ((0, 0), (0, 0), (0, BW - 3), (0, 0)))
    own = own.reshape(3 * joined_ch, BW * ocean_ch)
    gathered = lax.all_gather(own, "tile", axis=0)
    lead1, lead2 = atmosphere_leads(tile_count, rotations, atmosphere, conv_weight, conv_bias)
    return tuple(
        ocean_step(
            tile_count, rotations, lead1, lead2, ocean_state, land_sea[:, None], owners,
            force_weight, gathered,
        )
    )


def solution(mesh):
    in_specs = (
        P(("ens", "tile"), None, None),
        P(("ens", "tile"), None),
        P("tile"),
        P("tile", None),
        P(),
        P(),
        P(),
        P(),
        P("tile", None, None, None),
    )
    out_specs = (P(("ens", "tile"), None, None), P(("ens", "tile"), None))
    return jax.shard_map(
        functools.partial(local, mesh.shape["tile"]),
        mesh=mesh,
        in_specs=in_specs,
        out_specs=out_specs,
        check_vma=False,
    )
```

profile of v0, /device:TPU:1, one launch (start us, length us, event | category | flops | bytes accessed | tf_op | source)
XLA Modules:
  0.0 68.7 jit_solution(12804842965097153389)
XLA Ops:
  0.6 0.0 copy-start.6
  0.6 0.0 copy-start.7
  0.7 0.8 %copy.24.fw_ref = bf16[128,32]{1,0:T(8,128)(2,1)S(1)} copy(bf16[128,32]{0,1:T(8,128)(2,1)} %param.16) | data formatting | bytes 16384 | tf_op args[7]
  1.5 0.0 copy-done.6
  1.5 0.0 copy-start.5
  1.5 0.1 copy.22.land_ref
  1.6 0.0 copy-done.7
  1.6 0.1 copy.23.owner_ref
  1.7 0.6 copy-done.5
  2.4 0.0 copy-start.2
  2.4 0.1 copy.20
  2.5 0.1 pad.4
  2.5 0.1 all_gather_reshape.3
  2.7 0.0 copy-start.3
  2.7 0.1 copy.21
  2.8 0.0 copy-start.1
  2.8 0.0 copy-start.4
  2.8 25.5 %all_gather.3.v_ref = bf16[16,192,128]{2,1,0:T(8,128)(2,1)S(1)} all-gather(bf16[1,192,128]{2,1,0:T(8,128)(2,1)S(1)} %copy.21), channel_id=1, replica_groups=mesh['ens'=2,'tile'=16] {'tile'}, dimensions={0}, use_global_device_ids=true | all-gather | bytes 835584 | tf_op jit(solution)/shard_map/all_gather | solution.py:338
  28.3 0.0 copy-done.2
  28.3 0.0 copy-done.3
  28.3 0.0 copy-done.1
  28.3 0.0 copy-done.4
  28.3 0.0 copy-start
  28.3 33.5 %atmosphere.1 = (bf16[8,256,128]{2,1,0:T(8,128)(2,1)S(1)}, bf16[8,256,128]{2,1,0:T(8,128)(2,1)S(1)}) custom-call(s32[16]{0:T(128)S(1)} %copy-done.1, bf16[8,256,128]{2,1,0:T(8,128)(2,1)S(1)} %copy-done.3, bf16[3,9,128,128]{3,2,1,0:T(8,128)(2,1)S(1)} %copy-done.2, bf16[3,128]{1,0:T(4,128)(2,1)S(1)} %copy-done.4), custom_call_target="tpu_custom_call" | custom-call | flops 6643777536 | bytes 2097152 | tf_op jit(solution)/shard_map/atmosphere/pallas_call | solution.py:187
  61.8 0.0 copy-done
  61.8 6.8 %ocean.1 = (bf16[8,256,128]{2,1,0:T(8,128)(2,1)}, bf16[128,512]{1,0:T(8,128)(2,1)}) custom-call(s32[16]{0:T(128)S(1)} %copy-done.1, bf16[8,256,128]{2,1,0:T(8,128)(2,1)S(1)} %get-tuple-element.4.lead1_ref, bf16[8,256,128]{2,1,0:T(8,128)(2,1)S(1)} %get-tuple-element.5.lead2_ref, bf16[128,512]{1,0:T(8,128)(2,1)S(1)} %copy-done, s32[128,1]{1,0:T(8,128)S(1)} %copy.22.land_ref, ...), custom_call_target="tpu_custom_call" | custom-call | tf_op jit(solution)/shard_map/ocean/pallas_call | solution.py:312
  (1 shorter events, 0.0 us)
Async XLA Ops:
  0.6 0.8 %copy-start.6 = (s32[128]{0:T(128)S(1)}, s32[128]{0:T(128)}, u32[]{:S(2)}) copy-start(s32[128]{0:T(128)} %param.11) | copy-start | bytes 1540
  0.6 1.0 %copy-start.7 = (s32[128,1]{0,1:T(1,128)S(1)}, s32[128,1]{0,1:T(1,128)}, u32[]{:S(2)}) copy-start(s32[128,1]{0,1:T(1,128)} %param.12) | copy-start | bytes 1540
  1.5 0.9 %copy-start.5 = (bf16[1,9,64,32]{2,3,1,0:T(8,128)(2,1)S(1)}, bf16[1,9,64,32]{2,3,1,0:T(8,128)(2,1)}, u32[]{:S(2)}) copy-start(bf16[1,9,64,32]{2,3,1,0:T(8,128)(2,1)} %param.17) | copy-start | bytes 110596
  2.4 25.9 %copy-start.2 = (bf16[3,9,128,128]{3,2,1,0:T(8,128)(2,1)S(1)}, bf16[3,9,128,128]{3,2,1,0:T(8,128)(2,1)}, u32[]{:S(2)}) copy-start(bf16[3,9,128,128]{3,2,1,0:T(8,128)(2,1)} %w_ref.1) | copy-start | bytes 2654212
  2.7 25.6 %copy-start.3 = (bf16[8,256,128]{2,1,0:T(8,128)(2,1)S(1)}, bf16[8,256,128]{2,1,0:T(8,128)(2,1)}, u32[]{:S(2)}) copy-start(bf16[8,256,128]{2,1,0:T(8,128)(2,1)} %band_ref.1) | copy-start | bytes 1572868
  2.8 25.5 %copy-start.1 = (s32[16]{0:T(128)S(1)}, s32[16]{0:T(128)}, u32[]{:S(2)}) copy-start(s32[16]{0:T(128)} %rot_ref.3) | copy-start | bytes 196
  2.8 25.5 %copy-start.4 = (bf16[3,128]{1,0:T(4,128)(2,1)S(1)}, bf16[3,128]{1,0:T(4,128)(2,1)}, u32[]{:S(2)}) copy-start(bf16[3,128]{1,0:T(4,128)(2,1)} %bias_ref.1) | copy-start | bytes 2308
  28.3 33.5 %copy-start = (bf16[128,512]{1,0:T(8,128)(2,1)S(1)}, bf16[128,512]{1,0:T(8,128)(2,1)}, u32[]{:S(2)}) copy-start(bf16[128,512]{1,0:T(8,128)(2,1)} %state_ref.1) | copy-start | bytes 393220
where the time goes:
time: 68.9 us; the launch traced here: 68.7 us
  Pallas kernels  40.3 us (58%)
  blocking collectives  25.5 us (37%)
  local copies, waits for them, and re-layouts  2.12 us (3%)
  between operations  0.74 us (1%)
    pallas_call x1, Pallas kernels, atmosphere_leads(): pl.pallas_call(functools.partial(atmosphere_kernel, tile_count), out_shap...  33.5 us
    all_gather x1, blocking collectives, local(): gathered = lax.all_gather(own, 'tile', axis=0)  25.5 us
    pallas_call x1, Pallas kernels, ocean_step(): pl.pallas_call(functools.partial(ocean_kernel, tile_count), out_shape=[ja...  6.84 us
    unnamed x18, local copies, waits for them, and re-layouts  1.62 us

commit v1 on v0

--- a/solution.py
+++ b/solution.py
@@ -22,15 +22,26 @@
     return jnp.dot(matrix, values, preferred_element_type=jnp.float32).astype(jnp.bfloat16)
 
 
+def flipped(index, bit):
+    return index + (1 - 2 * (index // 2**bit % 2)) * 2**bit
+
+
+def reversed_bits(index, bits):
+    return sum(index // 2**s % 2 * 2 ** (bits - 1 - s) for s in range(bits))
+
+
 def atmosphere_kernel(
-    tile_count, rot_ref, band_ref, w_ref, bias_ref, lead1_ref, lead2_ref,
-    ext, mid1, mid2, taps, send_sem, recv_sem,
+    tile_count, rot_ref, band_ref, w_ref, bias_ref, own_ref, lead1_ref, lead2_ref, v_ref,
+    ext, mid1, mid2, taps, send_sem, recv_sem, v_send, v_recv,
 ):
     me = lax.axis_index("tile")
     rows, columns, channels = band_ref.shape
     has_up = me > 0
     has_down = me < tile_count - 1
     barrier = pltpu.get_barrier_semaphore()
+    bits = tile_count.bit_length() - 1
+    for s in range(1, bits):
+        pl.semaphore_signal(barrier, inc=1, device_id={"tile": flipped(me, s)})
 
     @pl.when(has_up)
     def _():
@@ -48,7 +59,28 @@
     for r in range(rows):
         ext[0, MARGIN + r] = moved(turn, band_ref[r])
 
-    pl.semaphore_wait(barrier, jnp.minimum(me, 1) + jnp.minimum(tile_count - 1 - me, 1))
+    place = reversed_bits(me, bits)
+    v_ref[place] = own_ref[...]
+    pl.semaphore_wait(
+        barrier, bits - 1 + jnp.minimum(me, 1) + jnp.minimum(tile_count - 1 - me, 1)
+    )
+
+    def doubling(stage):
+        size = 2**stage
+        block = v_ref.at[pl.ds(place // size * size, size)]
+        return pltpu.make_async_remote_copy(
+            src_ref=block,
+            dst_ref=block,
+            send_sem=v_send.at[stage],
+            recv_sem=v_recv.at[stage],
+            device_id={"tile": flipped(me, bits - 1 - stage)},
+        )
+
+    def advance(stage):
+        if 0 < stage <= bits:
+            doubling(stage - 1).wait()
+        if stage < bits:
+            doubling(stage).start()
 
     def copies(lead):
         up = pltpu.make_async_remote_copy(
@@ -119,6 +151,13 @@
         lax.fori_loop(0, out_rows // 2, pair, 0, unroll=2)
 
     start(0)
+    advance(0)
+    points = LEADS * LAYERS
+
+    def steps(point):
+        for stage in range(1, bits + 1):
+            if (stage - 1) * points // bits == point:
+                advance(stage)
 
     for index in range(LAYERS):
         for k in range(4):
@@ -162,8 +201,11 @@
 
     for lead in range(LEADS):
         finish(lead)
+        steps(lead * LAYERS)
         layer(0, lambda r, lead=lead: ext[lead, r], set_mid1, rows + 12, 6)
+        steps(lead * LAYERS + 1)
         layer(1, lambda r: mid1[r], set_mid2, rows + 8, 4)
+        steps(lead * LAYERS + 2)
         layer(2, lambda r: mid2[r], (set_lead1, set_lead2)[lead], rows, 0)
         if lead + 1 < LEADS:
             start(lead + 1)
@@ -180,15 +222,16 @@
             down.wait_send()
 
 
-def atmosphere_leads(tile_count, rotations, band, conv_weight, conv_bias):
+def atmosphere_leads(tile_count, rotations, band, conv_weight, conv_bias, own):
     rows, columns, channels = band.shape
     vmem = pl.BlockSpec(memory_space=pltpu.VMEM)
     extended = (rows + 2 * MARGIN, columns, channels)
     return pl.pallas_call(
         functools.partial(atmosphere_kernel, tile_count),
-        out_shape=[jax.ShapeDtypeStruct(band.shape, jnp.bfloat16)] * 2,
-        in_specs=[pl.BlockSpec(memory_space=pltpu.SMEM), vmem, vmem, vmem],
-        out_specs=[vmem, vmem],
+        out_shape=[jax.ShapeDtypeStruct(band.shape, jnp.bfloat16)] * 2
+        + [jax.ShapeDtypeStruct((tile_count, *own.shape), jnp.bfloat16)],
+        in_specs=[pl.BlockSpec(memory_space=pltpu.SMEM)] + [vmem] * 4,
+        out_specs=[vmem] * 3,
         scratch_shapes=[
             pltpu.VMEM((LEADS, *extended), jnp.bfloat16),
             pltpu.VMEM((rows + 12, columns, channels), jnp.bfloat16),
@@ -196,6 +239,8 @@
             pltpu.VMEM((LAYERS, 4 * channels, 6 * channels), jnp.bfloat16),
             pltpu.SemaphoreType.DMA((LEADS, 2)),
             pltpu.SemaphoreType.DMA((LEADS, 2)),
+            pltpu.SemaphoreType.DMA((tile_count.bit_length() - 1,)),
+            pltpu.SemaphoreType.DMA((tile_count.bit_length() - 1,)),
         ],
         compiler_params=pltpu.CompilerParams(
             collective_id=0, has_side_effects=True, vmem_limit_bytes=VMEM_LIMIT
@@ -206,7 +251,7 @@
             transcendentals=88 * columns * channels,
         ),
         name="atmosphere",
-    )(rotations, band, conv_weight, conv_bias)
+    )(rotations, band, conv_weight, conv_bias, own)
 
 
 def ocean_kernel(
@@ -214,6 +259,7 @@
     atmos_ref, sea_ref, lhs, rhs, total,
 ):
     me = lax.axis_index("tile")
+    bits = tile_count.bit_length() - 1
     rows, columns, channels = lead1_ref.shape
     blocks, width = state_ref.shape
     ocean_ch = fw_ref.shape[1]
@@ -285,8 +331,9 @@
                         pl.ds(ah * group + pc * ocean_ch, ocean_ch), pl.ds(half * group, group)
                     ] = turned[ah * ocean_ch : (ah + 1) * ocean_ch]
         y = jnp.dot(lhs[...], rhs[...], preferred_element_type=jnp.float32)
-        kept = jnp.where(owner == 2 * k, y[:, :group], total[...])
-        total[...] = jnp.where(owner == 2 * k + 1, y[:, group:], kept)
+        first = reversed_bits(2 * k, bits)
+        kept = jnp.where(owner == first, y[:, :group], total[...])
+        total[...] = jnp.where(owner == first + tile_count // 2, y[:, group:], kept)
         return carry
 
     lax.fori_loop(0, tile_count // 2, two_owners, 0)
@@ -335,8 +382,9 @@
     own = ocean_weight[0].reshape(3, 3, joined_ch, ocean_ch)[:, ::-1].transpose(0, 2, 1, 3)
     own = jnp.pad(own, ((0, 0), (0, 0), (0, BW - 3), (0, 0)))
     own = own.reshape(3 * joined_ch, BW * ocean_ch)
-    gathered = lax.all_gather(own, "tile", axis=0)
-    lead1, lead2 = atmosphere_leads(tile_count, rotations, atmosphere, conv_weight, conv_bias)
+    lead1, lead2, gathered = atmosphere_leads(
+        tile_count, rotations, atmosphere, conv_weight, conv_bias, own
+    )
     return tuple(
         ocean_step(
             tile_count, rotations, lead1, lead2, ocean_state, land_sea[:, None], owners,

time: 68.9 us -> 53.1 us (0.77)
  the two profiles are of different devices: /device:TPU:1 before, /device:TPU:11 now
where the time goes in v1:
time: 53.1 us; the launch traced here: 52.8 us
  Pallas kernels  46.8 us (88%)
  local copies, waits for them, and re-layouts  5.3 us (10%)
  between operations  0.7 us (1%)
    pallas_call x1, Pallas kernels, atmosphere_leads(): pl.pallas_call(functools.partial(atmosphere_kernel, tile_count), out_shap...  40 us
    pallas_call x1, Pallas kernels, ocean_step(): pl.pallas_call(functools.partial(ocean_kernel, tile_count), out_shape=[ja...  6.84 us
    unnamed x12, local copies, waits for them, and re-layouts  3.26 us

profile of v1, /device:TPU:11, one launch (start us, length us, event | category | flops | bytes accessed | tf_op | source)
XLA Modules:
  0.0 52.8 jit_solution(8934677473075533981)
XLA Ops:
  0.6 0.0 copy-start.2
  0.6 0.9 %copy.19.fw_ref = bf16[128,32]{1,0:T(8,128)(2,1)S(1)} copy(bf16[128,32]{0,1:T(8,128)(2,1)} %param.16) | data formatting | bytes 16384 | tf_op args[7]
  1.5 0.8 %copy.17.land_ref = s32[128,1]{1,0:T(8,128)S(1)} copy(s32[128,1]{0,1:T(1,128)} %bitcast.7) | data formatting | bytes 1024 | tf_op jit(solution)/shard_map/broadcast_in_dim | solution.py:390
  2.3 0.8 %copy.18.owner_ref = s32[128,1]{1,0:T(8,128)S(1)} copy(s32[128,1]{0,1:T(1,128)} %param.12) | data formatting | bytes 1024 | tf_op args[3]
  3.1 0.9 %copy.15 = bf16[3,3,64,32]{2,0,3,1:T(4,128)(2,1)S(1)} copy(bf16[3,3,64,32]{2,3,1,0:T(8,128)(2,1)} %bitcast.6) | data formatting | bytes 73728 | tf_op jit(solution)/shard_map/reshape;squeeze | solution.py:382
  4.0 0.1 pad.4
  4.1 0.1 reshape.7
  4.2 0.0 copy-start.1
  4.2 0.0 copy-start.4
  4.3 0.1 copy.16.own_ref
  4.4 0.0 copy-done.2
  4.4 0.5 copy-done.1
  4.9 0.0 copy-done.4
  4.9 0.0 copy-start.3
  4.9 1.0 %copy-done.3 = bf16[8,256,128]{2,1,0:T(8,128)(2,1)S(1)} copy-done((bf16[8,256,128]{2,1,0:T(8,128)(2,1)S(1)}, bf16[8,256,128]{2,1,0:T(8,128)(2,1)}, u32[]{:S(2)}) %copy-start.3) | copy-done | bytes 524312
  6.0 0.0 copy-start
  6.0 40.0 %atmosphere.1 = (bf16[8,256,128]{2,1,0:T(8,128)(2,1)S(1)}, bf16[8,256,128]{2,1,0:T(8,128)(2,1)S(1)}, bf16[16,192,128]{2,1,0:T(8,128)(2,1)S(1)}) custom-call(s32[16]{0:T(128)S(1)} %copy-done.1, bf16[8,256,128]{2,1,0:T(8,128)(2,1)S(1)} %copy-done.3, bf16[3,9,128,128]{3,2,1,0:T(8,128)(2,1)S(1)} %copy-done.2, bf16[3,128]{1,0:T(4,128)(2,1)S(1)} %copy-done.4, ...), custom_call_target="tpu_custom_call" | custom-call | flops 6643777536 | bytes 2097152 | tf_op jit(solution)/shard_map/atmosphere/pallas_call | solution.py:229
  46.0 0.0 copy-done
  46.0 6.8 %ocean.1 = (bf16[8,256,128]{2,1,0:T(8,128)(2,1)}, bf16[128,512]{1,0:T(8,128)(2,1)}) custom-call(s32[16]{0:T(128)S(1)} %copy-done.1, bf16[8,256,128]{2,1,0:T(8,128)(2,1)S(1)} %get-tuple-element.5.lead1_ref, bf16[8,256,128]{2,1,0:T(8,128)(2,1)S(1)} %get-tuple-element.6.lead2_ref, bf16[128,512]{1,0:T(8,128)(2,1)S(1)} %copy-done, s32[128,1]{1,0:T(8,128)S(1)} %copy.17.land_ref, ...), custom_call_target="tpu_custom_call" | custom-call | tf_op jit(solution)/shard_map/ocean/pallas_call | solution.py:359
  (1 shorter events, 0.0 us)
Async XLA Ops:
  0.6 3.7 %copy-start.2 = (bf16[3,9,128,128]{3,2,1,0:T(8,128)(2,1)S(1)}, bf16[3,9,128,128]{3,2,1,0:T(8,128)(2,1)}, u32[]{:S(2)}) copy-start(bf16[3,9,128,128]{3,2,1,0:T(8,128)(2,1)} %w_ref.1) | copy-start | bytes 2654212
  4.2 0.7 %copy-start.1 = (s32[16]{0:T(128)S(1)}, s32[16]{0:T(128)}, u32[]{:S(2)}) copy-start(s32[16]{0:T(128)} %rot_ref.3) | copy-start | bytes 196
  4.2 0.7 %copy-start.4 = (bf16[3,128]{1,0:T(4,128)(2,1)S(1)}, bf16[3,128]{1,0:T(4,128)(2,1)}, u32[]{:S(2)}) copy-start(bf16[3,128]{1,0:T(4,128)(2,1)} %bias_ref.1) | copy-start | bytes 2308
  4.9 1.0 %copy-start.3 = (bf16[8,256,128]{2,1,0:T(8,128)(2,1)S(1)}, bf16[8,256,128]{2,1,0:T(8,128)(2,1)}, u32[]{:S(2)}) copy-start(bf16[8,256,128]{2,1,0:T(8,128)(2,1)} %band_ref.1) | copy-start | bytes 1572868
  6.0 40.0 %copy-start = (bf16[128,512]{1,0:T(8,128)(2,1)S(1)}, bf16[128,512]{1,0:T(8,128)(2,1)}, u32[]{:S(2)}) copy-start(bf16[128,512]{1,0:T(8,128)(2,1)} %state_ref.1) | copy-start | bytes 393220

commit v2 on v1

v2 whole, which is shorter than its diff:
```python
import functools
import jax
import jax.numpy as jnp
from jax import lax
from jax.experimental import pallas as pl
from jax.experimental.pallas import tpu as pltpu
from jax.sharding import PartitionSpec as P

LEADS = 2
LAYERS = 3
BH = 4
BW = 4
MARGIN = 2**LAYERS - 1
VMEM_LIMIT = 48 * 1024 * 1024


def one_hot(mask):
    return jnp.where(mask, 1.0, 0.0).astype(jnp.bfloat16)


def moved(matrix, values):
    return jnp.dot(matrix, values, preferred_element_type=jnp.float32).astype(jnp.bfloat16)


def flipped(index, bit):
    return index + (1 - 2 * (index // 2**bit % 2)) * 2**bit


def reversed_bits(index, bits):
    return sum(index // 2**s % 2 * 2 ** (bits - 1 - s) for s in range(bits))


GROUPS = ((1, 1), (2, 3), (4, 5), (6, 7))
WAVES = (
    ((0, 6), (0, 12)),
    ((0, 4), (0, 14), (1, 4), (1, 5), (1, 8), (1, 9)),
    ((0, 2), (0, 16)),
    ((0, 0), (0, 18), (1, 0), (1, 1), (1, 12), (1, 13)),
)
INTERIOR = ((0, 8), (0, 10))


def atmosphere_kernel(
    tile_count, rot_ref, band_ref, w_ref, bias_ref, ow_ref, leads_ref, v_ref,
    ext, mid1, mid2, taps, send_sem, recv_sem, v_send, v_recv,
):
    me = lax.axis_index("tile")
    rows, columns, channels = band_ref.shape
    has_up = me > 0
    has_down = me < tile_count - 1
    barrier = pltpu.get_barrier_semaphore()
    bits = tile_count.bit_length() - 1
    for s in range(1, bits):
        pl.semaphore_signal(barrier, inc=1, device_id={"tile": flipped(me, s)})

    @pl.when(has_up)
    def _():
        pl.semaphore_signal(barrier, inc=1, device_id={"tile": me - 1})

    @pl.when(has_down)
    def _():
        pl.semaphore_signal(barrier, inc=1, device_id={"tile": me + 1})

    shift = rot_ref[me]
    to = lax.broadcasted_iota(jnp.int32, (columns, columns), 0)
    source = lax.broadcasted_iota(jnp.int32, (columns, columns), 1)
    distance = source - to + shift
    turn = one_hot((distance == 0) | (distance == columns))

    def turn_rows(*which):
        for r in which:
            ext[0, MARGIN + r] = moved(turn, band_ref[r])

    def up_copy(lead, group):
        near, far = GROUPS[group]
        return pltpu.make_async_remote_copy(
            src_ref=ext.at[lead, pl.ds(MARGIN + near - 1, far - near + 1)],
            dst_ref=ext.at[lead, pl.ds(MARGIN + rows + near - 1, far - near + 1)],
            send_sem=send_sem.at[lead, 0, group],
            recv_sem=recv_sem.at[lead, 0, group],
            device_id={"tile": me - 1},
        )

    def down_copy(lead, group):
        near, far = GROUPS[group]
        return pltpu.make_async_remote_copy(
            src_ref=ext.at[lead, pl.ds(MARGIN + rows - far, far - near + 1)],
            dst_ref=ext.at[lead, pl.ds(MARGIN - far, far - near + 1)],
            send_sem=send_sem.at[lead, 1, group],
            recv_sem=recv_sem.at[lead, 1, group],
            device_id={"tile": me + 1},
        )

    def start(lead, *groups, also=True):
        @pl.when(has_up & also)
        def _():
            for group in groups:
                up_copy(lead, group).start()

        @pl.when(has_down & also)
        def _():
            for group in groups:
                down_copy(lead, group).start()

    def arrive(lead, group):
        @pl.when(has_up)
        def _():
            down_copy(lead, group).wait_recv()

        @pl.when(has_down)
        def _():
            up_copy(lead, group).wait_recv()

    place = reversed_bits(me, bits)

    def doubling(stage):
        size = 2**stage
        block = v_ref.at[pl.ds(place // size * size, size)]
        return pltpu.make_async_remote_copy(
            src_ref=block,
            dst_ref=block,
            send_sem=v_send.at[stage],
            recv_sem=v_recv.at[stage],
            device_id={"tile": flipped(me, bits - 1 - stage)},
        )

    def advance(stage):
        if 0 < stage <= bits:
            doubling(stage - 1).wait()
        if stage < bits:
            doubling(stage).start()

    def pair(lead, index, r):
        dilation = 2**index
        margin_left = (6, 4, 0)[index]
        bias = bias_ref[index : index + 1, :].astype(jnp.float32)
        field = (ext.at[lead], mid1, mid2)[index]
        lhs = jnp.concatenate([field[r + k * dilation] for k in range(4)], axis=1)
        y = jnp.dot(lhs, taps[index], preferred_element_type=jnp.float32)
        for o in range(2):
            base = o * 3 * channels
            sums = (
                pltpu.roll(y[:, base : base + channels], dilation, 0)
                + y[:, base + channels : base + 2 * channels]
                + pltpu.roll(
                    y[:, base + 2 * channels : base + 3 * channels], columns - dilation, 0
                )
            )
            row = r + o * dilation
            centre = lhs[:, (1 + o) * channels : (2 + o) * channels].astype(jnp.float32)
            value = centre + jax.nn.gelu(sums + bias)
            if row < margin_left or row >= margin_left + rows:
                value = jnp.where(has_up if row < margin_left else has_down, value, 0.0)
            value = value.astype(jnp.bfloat16)
            if index == 0:
                mid1[row] = value
            elif index == 1:
                mid2[row] = value
            else:
                leads_ref[lead, row] = value
                ext[lead + 1, MARGIN + row] = value

    turn_rows(0, rows - 1)
    pl.semaphore_wait(
        barrier, bits - 1 + jnp.minimum(me, 1) + jnp.minimum(tile_count - 1 - me, 1)
    )
    start(0, 0)
    turn_rows(1, 2, 5, 6)
    start(0, 1)
    turn_rows(3, 4)
    start(0, 2, 3)

    for a in range(3):
        parts = [ow_ref[a * 3 + b].astype(jnp.float32) for b in (2, 1, 0)]
        parts = jnp.concatenate(parts + [jnp.zeros_like(parts[0])], axis=0)
        v_ref[place, pl.ds(a * parts.shape[1], parts.shape[1]), :] = parts.T.astype(jnp.bfloat16)
    advance(0)

    for index in range(LAYERS):
        for k in range(4):
            for o in range(2):
                for b in range(3):
                    a = k - o
                    where = (
                        index,
                        pl.ds(k * channels, channels),
                        pl.ds((o * 3 + b) * channels, channels),
                    )
                    if 0 <= a <= 2:
                        taps[where] = w_ref[index, a * 3 + b]
                    else:
                        taps[where] = jnp.zeros((channels, channels), jnp.bfloat16)

    @pl.when(jnp.logical_not(has_up))
    def _():
        for lead in range(LEADS):
            for r in range(MARGIN):
                ext[lead, r] = jnp.zeros((columns, channels), jnp.bfloat16)

    @pl.when(jnp.logical_not(has_down))
    def _():
        for lead in range(LEADS):
            for r in range(MARGIN):
                ext[lead, MARGIN + rows + r] = jnp.zeros((columns, channels), jnp.bfloat16)

    points = LEADS * len(GROUPS)

    def one_lead(lead, carry):
        for index, r in INTERIOR:
            pair(lead, index, r)
        for group in range(len(GROUPS)):
            arrive(lead, group)
            for stage in range(1, bits + 1):
                point = (stage - 1) * points // bits
                if point % len(GROUPS) == group:

                    @pl.when(lead == point // len(GROUPS))
                    def _(stage=stage):
                        advance(stage)

            for index, r in WAVES[group]:
                pair(lead, index, r)
        more = lead + 1 < LEADS
        pair(lead, 2, 0)
        pair(lead, 2, 3)
        start(lead + 1, 0, also=more)
        pair(lead, 2, 1)
        pair(lead, 2, 2)
        start(lead + 1, 1, 2, 3, also=more)
        return carry

    lax.fori_loop(0, LEADS, one_lead, 0)

    for lead in range(LEADS):

        @pl.when(has_up)
        def _(lead=lead):
            for group in range(len(GROUPS)):
                up_copy(lead, group).wait_send()

        @pl.when(has_down)
        def _(lead=lead):
            for group in range(len(GROUPS)):
                down_copy(lead, group).wait_send()


def atmosphere_leads(tile_count, rotations, band, conv_weight, conv_bias, ocean_weight):
    rows, columns, channels = band.shape
    vmem = pl.BlockSpec(memory_space=pltpu.VMEM)
    extended = (rows + 2 * MARGIN, columns, channels)
    ocean_ch, joined_ch = ocean_weight.shape[1:]
    gathered = (tile_count, 3 * joined_ch, BW * ocean_ch)
    return pl.pallas_call(
        functools.partial(atmosphere_kernel, tile_count),
        out_shape=[
            jax.ShapeDtypeStruct((LEADS, *band.shape), jnp.bfloat16),
            jax.ShapeDtypeStruct(gathered, jnp.bfloat16),
        ],
        in_specs=[pl.BlockSpec(memory_space=pltpu.SMEM)] + [vmem] * 4,
        out_specs=[vmem] * 2,
        scratch_shapes=[
            pltpu.VMEM((LEADS + 1, *extended), jnp.bfloat16),
            pltpu.VMEM((rows + 12, columns, channels), jnp.bfloat16),
            pltpu.VMEM((rows + 8, columns, channels), jnp.bfloat16),
            pltpu.VMEM((LAYERS, 4 * channels, 6 * channels), jnp.bfloat16),
            pltpu.SemaphoreType.DMA((LEADS, 2, len(GROUPS))),
            pltpu.SemaphoreType.DMA((LEADS, 2, len(GROUPS))),
            pltpu.SemaphoreType.DMA((tile_count.bit_length() - 1,)),
            pltpu.SemaphoreType.DMA((tile_count.bit_length() - 1,)),
        ],
        compiler_params=pltpu.CompilerParams(
            collective_id=0, has_side_effects=True, vmem_limit_bytes=VMEM_LIMIT
        ),
        cost_estimate=pl.CostEstimate(
            flops=2 * 88 * columns * 9 * channels * channels,
            bytes_accessed=4 * rows * columns * channels * 2,
            transcendentals=88 * columns * channels,
        ),
        name="atmosphere",
    )(rotations, band, conv_weight, conv_bias, ocean_weight)


def ocean_kernel(
    tile_count, rot_ref, leads_ref, state_ref, land_ref, owner_ref, fw_ref, v_ref,
    atmos_ref, sea_ref, lhs, rhs, total,
):
    me = lax.axis_index("tile")
    bits = tile_count.bit_length() - 1
    rows, columns, channels = leads_ref.shape[1:]
    blocks, width = state_ref.shape
    ocean_ch = fw_ref.shape[0]
    cells = BH * BW
    group = BW * ocean_ch
    across = columns // BW
    shift = rot_ref[me]

    to = lax.broadcasted_iota(jnp.int32, (columns, columns), 0)
    source = lax.broadcasted_iota(jnp.int32, (columns, columns), 1)
    distance = to + shift - source
    back = one_hot((distance == 0) | (distance == columns))
    for r in range(rows):
        atmos_ref[r] = moved(back, leads_ref[1, r])

    distance = (to % across) * BW + to // across + shift - source
    gather = one_hot((distance == 0) | (distance == columns))
    fw4 = jnp.concatenate([fw_ref[...].astype(jnp.float32)] * BW, axis=0).T.astype(jnp.bfloat16)

    s = lax.broadcasted_iota(jnp.int32, (width, width), 0)
    t = lax.broadcasted_iota(jnp.int32, (width, width), 1)
    permute = one_hot((s // cells == t % ocean_ch) & (s % cells == t // ocean_ch))
    state = moved(state_ref[...], permute)

    piece_lane = lax.broadcasted_iota(jnp.int32, (across, group), 1) // ocean_ch
    lhs[...] = jnp.zeros_like(lhs)
    wide = 2 * group
    for r in range(rows):
        i, pr = r // BH, r % BH
        forcing = 0.5 * (
            jnp.dot(leads_ref[0, r], fw4, preferred_element_type=jnp.float32)
            + jnp.dot(leads_ref[1, r], fw4, preferred_element_type=jnp.float32)
        )
        y = jnp.dot(gather, forcing.astype(jnp.bfloat16), preferred_element_type=jnp.float32)
        piece = jnp.zeros((across, group), jnp.float32)
        for pc in range(BW):
            piece = jnp.where(piece_lane == pc, y[pc * across : (pc + 1) * across], piece)
        piece = piece.astype(jnp.bfloat16)
        for a in range(3):
            q = pr + 1 - a
            if 0 <= q < BH:
                lhs[pl.ds(q * blocks + i * across, across), pl.ds(a * wide, group)] = piece
    for pr in range(BH):
        for a in range(3):
            q = pr + 1 - a
            if 0 <= q < BH:
                lhs[pl.ds(q * blocks, blocks), pl.ds(a * wide + group, group)] = state[
                    :, pr * group : (pr + 1) * group
                ]

    owner = jnp.broadcast_to(owner_ref[...].astype(jnp.float32), (group, blocks)).T
    owner = jnp.concatenate([owner] * BH, axis=0)
    total[...] = jnp.zeros_like(total)
    v_lane = lax.broadcasted_iota(jnp.int32, (v_ref.shape[1], group), 1) // ocean_ch

    def two_owners(k, carry):
        for half in range(2):
            v = v_ref[2 * k + half].astype(jnp.float32)
            for pc in range(BW):
                turned = v if pc == 1 else pltpu.roll(v, ((pc - 1) * ocean_ch) % group, 1)
                if pc == 0:
                    turned = jnp.where(v_lane == BW - 1, 0.0, turned)
                if pc > 2:
                    turned = jnp.where(v_lane < pc - 1, 0.0, turned)
                turned = turned.astype(jnp.bfloat16)
                for ah in range(6):
                    rhs[
                        pl.ds(ah * group + pc * ocean_ch, ocean_ch), pl.ds(half * group, group)
                    ] = turned[ah * ocean_ch : (ah + 1) * ocean_ch]
        y = jnp.dot(lhs[...], rhs[...], preferred_element_type=jnp.float32)
        first = reversed_bits(2 * k, bits).astype(jnp.float32)
        kept = jnp.where(owner == first, y[:, :group], total[...])
        total[...] = jnp.where(owner == first + tile_count // 2, y[:, group:], kept)
        return carry

    lax.fori_loop(0, tile_count // 2, two_owners, 0)

    sea = jnp.broadcast_to(land_ref[...].astype(jnp.float32), (group, blocks)).T > 0
    out = jnp.zeros((blocks, width), jnp.float32)
    t = lax.broadcasted_iota(jnp.int32, (group, width), 0)
    s = lax.broadcasted_iota(jnp.int32, (group, width), 1)
    for q in range(BH):
        old = state[:, q * group : (q + 1) * group].astype(jnp.float32)
        new = old + jax.nn.gelu(total[pl.ds(q * blocks, blocks), :])
        new = jnp.where(sea, new, 0.0).astype(jnp.bfloat16)
        tq = t + q * group
        unpermute = one_hot((s // cells == tq % ocean_ch) & (s % cells == tq // ocean_ch))
        out = out + jnp.dot(new, unpermute, preferred_element_type=jnp.float32)
    sea_ref[...] = out.astype(jnp.bfloat16)


def ocean_step(tile_count, rotations, leads, state, land, owners, force_weight, gathered):
    vmem = pl.BlockSpec(memory_space=pltpu.VMEM)
    blocks = state.shape[0]
    group = BW * force_weight.shape[0]
    return pl.pallas_call(
        functools.partial(ocean_kernel, tile_count),
        out_shape=[
            jax.ShapeDtypeStruct(leads.shape[1:], jnp.bfloat16),
            jax.ShapeDtypeStruct(state.shape, jnp.bfloat16),
        ],
        in_specs=[pl.BlockSpec(memory_space=pltpu.SMEM)] + [vmem] * 6,
        out_specs=[vmem, vmem],
        scratch_shapes=[
            pltpu.VMEM((BH * blocks, 6 * group), jnp.bfloat16),
            pltpu.VMEM((6 * group, 2 * group), jnp.bfloat16),
            pltpu.VMEM((BH * blocks, group), jnp.float32),
        ],
        compiler_params=pltpu.CompilerParams(vmem_limit_bytes=VMEM_LIMIT),
        name="ocean",
    )(rotations, leads, state, land, owners, force_weight, gathered)


def local(
    tile_count, atmosphere, ocean_state, land_sea, owners, rotations, conv_weight, conv_bias,
    force_weight, ocean_weight,
):
    leads, gathered = atmosphere_leads(
        tile_count, rotations, atmosphere, conv_weight, conv_bias,
        ocean_weight[0].transpose(0, 2, 1),
    )
    return tuple(
        ocean_step(
            tile_count, rotations, leads, ocean_state, land_sea[None, :], owners.T,
            force_weight.T, gathered,
        )
    )


def solution(mesh):
    in_specs = (
        P(("ens", "tile"), None, None),
        P(("ens", "tile"), None),
        P("tile"),
        P("tile", None),
        P(),
        P(),
        P(),
        P(),
        P("tile", None, None, None),
    )
    out_specs = (P(("ens", "tile"), None, None), P(("ens", "tile"), None))
    return jax.shard_map(
        functools.partial(local, mesh.shape["tile"]),
        mesh=mesh,
        in_specs=in_specs,
        out_specs=out_specs,
        check_vma=False,
    )
```

time: 53.1 us -> 47 us (0.89)
  the two profiles are of different devices: /device:TPU:11 before, /device:TPU:0 now
where the time goes in v2:
time: 47 us; the launch traced here: 46.7 us
  Pallas kernels  41.6 us (89%)
  local copies, waits for them, and re-layouts  4.42 us (9%)
  between operations  0.69 us (1%)
    pallas_call x1, Pallas kernels, atmosphere_leads(): pl.pallas_call(functools.partial(atmosphere_kernel, tile_count), out_shap...  34.8 us
    pallas_call x1, Pallas kernels, ocean_step(): pl.pallas_call(functools.partial(ocean_kernel, tile_count), out_shape=[ja...  6.76 us
    unnamed x18, local copies, waits for them, and re-layouts  4.42 us

profile of v2, /device:TPU:0, one launch (start us, length us, event | category | flops | bytes accessed | tf_op | source)
XLA Modules:
  0.0 46.7 jit_solution(17099685417576981225)
XLA Ops:
  0.6 0.0 copy-start.2
  0.6 0.0 copy-start.8
  0.7 0.6 %copy-done.2 = s32[16]{0:T(128)S(1)} copy-done((s32[16]{0:T(128)S(1)}, s32[16]{0:T(128)}, u32[]{:S(2)}) %copy-start.2) | copy-done | bytes 88
  1.3 0.0 copy-done.8
  1.3 0.0 copy-start.5
  1.3 1.2 %copy-done.5 = bf16[3,9,128,128]{3,2,1,0:T(8,128)(2,1)S(1)} copy-done((bf16[3,9,128,128]{3,2,1,0:T(8,128)(2,1)S(1)}, bf16[3,9,128,128]{3,2,1,0:T(8,128)(2,1)}, u32[]{:S(2)}) %copy-start.5) | copy-done | bytes 884760
  2.5 0.0 copy-start.6
  2.5 1.0 %copy-done.6 = bf16[8,256,128]{2,1,0:T(8,128)(2,1)S(1)} copy-done((bf16[8,256,128]{2,1,0:T(8,128)(2,1)S(1)}, bf16[8,256,128]{2,1,0:T(8,128)(2,1)}, u32[]{:S(2)}) %copy-start.6) | copy-done | bytes 524312
  3.5 0.0 copy-start.7
  3.5 0.9 %copy-done.7 = bf16[1,9,64,32]{2,3,1,0:T(8,128)(2,1)S(1)} copy-done((bf16[1,9,64,32]{2,3,1,0:T(8,128)(2,1)S(1)}, bf16[1,9,64,32]{2,3,1,0:T(8,128)(2,1)}, u32[]{:S(2)}) %copy-start.7) | copy-done | bytes 36888
  4.4 0.0 copy-start
  4.4 0.0 copy-start.1
  4.4 34.8 %atmosphere.1 = (bf16[2,8,256,128]{3,2,1,0:T(8,128)(2,1)S(1)}, bf16[16,192,128]{2,1,0:T(8,128)(2,1)S(1)}) custom-call(s32[16]{0:T(128)S(1)} %copy-done.2, bf16[8,256,128]{2,1,0:T(8,128)(2,1)S(1)} %copy-done.6, bf16[3,9,128,128]{3,2,1,0:T(8,128)(2,1)S(1)} %copy-done.5, bf16[3,128]{1,0:T(4,128)(2,1)S(1)} %copy-done.8, bf16[9,32,64]{2,1,0:T(8,128)(2,1)S(1)} %bitcast.9), custom_call_target="tpu_custom_call" | custom-call | flops 6643777536 | bytes 2097152 | tf_op jit(solution)/shard_map/atmosphere/pallas_call | solution.py:253
  39.3 0.0 copy-start.3
  39.3 0.0 copy-start.4
  39.3 0.0 copy-done
  39.3 0.0 copy-done.1
  39.3 0.6 %copy-done.3 = s32[128]{0:T(128)S(1)} copy-done((s32[128]{0:T(128)S(1)}, s32[128]{0:T(128)}, u32[]{:S(2)}) %copy-start.3) | copy-done | bytes 536
  39.9 0.0 copy-done.4
  39.9 6.8 %ocean.1 = (bf16[8,256,128]{2,1,0:T(8,128)(2,1)}, bf16[128,512]{1,0:T(8,128)(2,1)}) custom-call(s32[16]{0:T(128)S(1)} %copy-done.2, bf16[2,8,256,128]{3,2,1,0:T(8,128)(2,1)S(1)} %get-tuple-element.4.leads_ref, bf16[128,512]{1,0:T(8,128)(2,1)S(1)} %copy-done, s32[1,128]{1,0:T(1,128)S(1)} %bitcast.7, s32[1,128]{1,0:T(1,128)S(1)} %bitcast.8, ...), custom_call_target="tpu_custom_call" | custom-call | tf_op jit(solution)/shard_map/ocean/pallas_call | solution.py:384
Async XLA Ops:
  0.6 0.7 %copy-start.2 = (s32[16]{0:T(128)S(1)}, s32[16]{0:T(128)}, u32[]{:S(2)}) copy-start(s32[16]{0:T(128)} %rot_ref.3) | copy-start | bytes 196
  0.6 0.7 %copy-start.8 = (bf16[3,128]{1,0:T(4,128)(2,1)S(1)}, bf16[3,128]{1,0:T(4,128)(2,1)}, u32[]{:S(2)}) copy-start(bf16[3,128]{1,0:T(4,128)(2,1)} %bias_ref.1) | copy-start | bytes 2308
  1.3 1.2 %copy-start.5 = (bf16[3,9,128,128]{3,2,1,0:T(8,128)(2,1)S(1)}, bf16[3,9,128,128]{3,2,1,0:T(8,128)(2,1)}, u32[]{:S(2)}) copy-start(bf16[3,9,128,128]{3,2,1,0:T(8,128)(2,1)} %w_ref.1) | copy-start | bytes 2654212
  2.5 1.0 %copy-start.6 = (bf16[8,256,128]{2,1,0:T(8,128)(2,1)S(1)}, bf16[8,256,128]{2,1,0:T(8,128)(2,1)}, u32[]{:S(2)}) copy-start(bf16[8,256,128]{2,1,0:T(8,128)(2,1)} %band_ref.1) | copy-start | bytes 1572868
  3.5 0.9 %copy-start.7 = (bf16[1,9,64,32]{2,3,1,0:T(8,128)(2,1)S(1)}, bf16[1,9,64,32]{2,3,1,0:T(8,128)(2,1)}, u32[]{:S(2)}) copy-start(bf16[1,9,64,32]{2,3,1,0:T(8,128)(2,1)} %param.17) | copy-start | bytes 110596
  4.4 34.9 %copy-start = (bf16[128,512]{1,0:T(8,128)(2,1)S(1)}, bf16[128,512]{1,0:T(8,128)(2,1)}, u32[]{:S(2)}) copy-start(bf16[128,512]{1,0:T(8,128)(2,1)} %state_ref.1) | copy-start | bytes 393220
  4.4 34.9 %copy-start.1 = (bf16[128,32]{0,1:T(8,128)(2,1)S(1)}, bf16[128,32]{0,1:T(8,128)(2,1)}, u32[]{:S(2)}) copy-start(bf16[128,32]{0,1:T(8,128)(2,1)} %param.16) | copy-start | bytes 24580
  39.3 0.7 %copy-start.3 = (s32[128]{0:T(128)S(1)}, s32[128]{0:T(128)}, u32[]{:S(2)}) copy-start(s32[128]{0:T(128)} %param.11) | copy-start | bytes 1540
  39.3 0.7 %copy-start.4 = (s32[128,1]{0,1:T(1,128)S(1)}, s32[128,1]{0,1:T(1,128)}, u32[]{:S(2)}) copy-start(s32[128,1]{0,1:T(1,128)} %param.12) | copy-start | bytes 1540
